TPU v7x, 512 devices: a whole 4x8x8 slice. The times are simulated.
512 devices in a mesh: vocab: 16 (over y, core), docs: 32 (over x, z).
Axes of the slice: x: 4, y: 8, z: 8, core: 2. Of those that a mesh axis runs over, the one named last changes fastest.
Arguments:
- counts: bfloat16 [65536, 4, 128], P(('vocab', 'docs')), may hold values from 0 to 2
- doc_owner: int32 [65536, 4], P(('vocab', 'docs')), may hold values from 0 to 511, all different within a row; in each aligned block of 128 rows (0 to 127, 128 to 255, ...) at most 2 rows name the same one
- doc_sub: int32 [65536, 4], P(('vocab', 'docs')), may hold values from 0 to 7
- doc_len: int32 [65536], P(('vocab', 'docs')), may hold values from 256 to 1023
- first_weight: bfloat16 [524288, 2048], P(('vocab', 'docs')), may hold values from -0.25 to 0.25
- first_bias: float32 [2048], replicated, may hold values from -3 to 3
- head_weight: bfloat16 [2048, 1536], P('vocab', 'docs'), may hold values from -0.125 to 0.125
- head_bias: float32 [1536], replicated, may hold values from -4 to 4
- factor: bfloat16 [1536, 1536], P('vocab', 'docs'), as said below
- noise_draw: bfloat16 [65536, 1536], P(('vocab', 'docs')), may hold values from -5 to 5
Outputs:
- sample: bfloat16 [65536, 1536], P(('vocab', 'docs'))
Inputs may be any that keep to these rules, and one draw needn't show every extreme that they name: `doc_owner`: each document names 4 different owners. The documents of one device name one owner in at most 2 slots, and on some device some owner is named in exactly 2 slots. `factor`: lower triangular; diagonal entries lie between 0.5 and 1.5.
All inputs are finite; a program needn't handle non-finite values.
Results may differ from a plain program's by a relative error of at most 0.0038.
Values may be sent and summed in bfloat16 or wider, within the bound.
No kernel may reach another device: no remote copies, remote signals or barrier semaphores. Data moves between devices by JAX's collectives and lax.ppermute only.
A program may use at most 128 MiB of HBM per device.

v0:
```python
import jax
import jax.numpy as jnp
from jax import lax
from jax.sharding import PartitionSpec as P


def local(
    counts,
    doc_owner,
    doc_sub,
    doc_len,
    first_weight,
    first_bias,
    head_weight,
    head_bias,
    factor,
    noise_draw,
):
    vocab_devices = lax.axis_size("vocab")
    docs_devices = lax.axis_size("docs")
    device_count = vocab_devices * docs_devices
    docs_here, slot_count, block_width = counts.shape
    hidden_width = first_weight.shape[1]
    per_owner = first_weight.shape[0] // block_width
    capacity = max(2, 2 * docs_here * slot_count // device_count)
    owner_flat = doc_owner.reshape(-1)
    onehot = (owner_flat[:, None] == jnp.arange(device_count, dtype=jnp.int32)[None, :]).astype(
        jnp.int32
    )
    position = jnp.sum(jnp.cumsum(onehot, axis=0) * onehot, axis=1) - 1
    slot_index = owner_flat * capacity + position
    flat_rows = counts.reshape(-1, block_width)
    send_rows = (
        jnp.zeros((device_count * capacity, block_width), counts.dtype)
        .at[slot_index]
        .set(flat_rows)
    )
    send_sub = (
        jnp.zeros((device_count * capacity,), jnp.bfloat16)
        .at[slot_index]
        .set(doc_sub.reshape(-1).astype(jnp.bfloat16))
    )
    send_rows = send_rows.reshape(vocab_devices, docs_devices, capacity, block_width)
    send_sub = send_sub.reshape(vocab_devices, docs_devices, capacity)
    got_rows, got_sub = (
        lax.all_to_all(
            lax.all_to_all(send_rows, "vocab", split_axis=0, concat_axis=0, tiled=True),
            "docs",
            split_axis=1,
            concat_axis=1,
            tiled=True,
        ),
        lax.all_to_all(
            lax.all_to_all(send_sub, "vocab", split_axis=0, concat_axis=0, tiled=True),
            "docs",
            split_axis=1,
            concat_axis=1,
            tiled=True,
        ),
    )
    got_rows = got_rows.reshape(-1, block_width)
    got_sub = got_sub.reshape(-1).astype(jnp.int32)
    select = (got_sub[:, None] == jnp.arange(per_owner, dtype=jnp.int32)[None, :]).astype(
        jnp.bfloat16
    )
    spread = (select[:, :, None] * got_rows[:, None, :]).reshape(-1, per_owner * block_width)
    owner_terms = jnp.dot(spread, first_weight, preferred_element_type=jnp.float32).astype(
        jnp.bfloat16
    )
    owner_terms = owner_terms.reshape(vocab_devices, docs_devices, capacity, hidden_width)
    returned = lax.all_to_all(
        lax.all_to_all(owner_terms, "vocab", split_axis=0, concat_axis=0, tiled=True),
        "docs",
        split_axis=1,
        concat_axis=1,
        tiled=True,
    )
    returned = returned.reshape(-1, hidden_width)
    own_rows = returned[slot_index].reshape(docs_here, slot_count, hidden_width).astype(jnp.float32)
    summed = jnp.sum(own_rows, axis=1)
    length_scale = 128.0 * slot_count / doc_len.astype(jnp.float32)
    hidden = jax.nn.softplus(summed * length_scale[:, None] + first_bias).astype(jnp.bfloat16)
    panel_rows = lax.all_gather(head_weight, "docs", axis=1, tiled=True)
    location = jnp.dot(
        hidden,
        lax.all_gather(panel_rows, "vocab", axis=0, tiled=True),
        preferred_element_type=jnp.float32,
    )
    factor_panel = lax.all_gather(factor, "docs", axis=1, tiled=True)
    correlated = lax.dot_general(
        noise_draw,
        lax.all_gather(factor_panel, "vocab", axis=0, tiled=True),
        (((1,), (1,)), ((), ())),
        preferred_element_type=jnp.float32,
    )
    return (location + head_bias + correlated).astype(jnp.bfloat16)


def solution(mesh):
    return jax.shard_map(
        local,
        mesh=mesh,
        in_specs=(
            P(("vocab", "docs"), None, None),
            P(("vocab", "docs"), None),
            P(("vocab", "docs"), None),
            P(("vocab", "docs")),
            P(("vocab", "docs"), None),
            P(),
            P("vocab", "docs"),
            P(),
            P("vocab", "docs"),
            P(("vocab", "docs"), None),
        ),
        out_specs=P(("vocab", "docs"), None),
        check_vma=False,
    )
```

profile of v0, /device:TPU:1, one launch (start us, length us, event | category | flops | bytes accessed | tf_op | source)
XLA Modules:
  0.0 425.2 jit_solution(10619048773508162734)
XLA Ops:
  6.5 50.0 %all_gather.12 = bf16[128,1536]{0,1:T(8,128)(2,1)} all-gather(bf16[128,48]{0,1:T(8,128)(2,1)} %param.16), channel_id=1, replica_groups=mesh['vocab'=16,'docs'=32] {'docs'}, dimensions={1}, use_global_device_ids=true | all-gather | bytes 405504 | tf_op jit(solution)/shard_map/all_gather | solution.py:83
  56.6 0.8 copy.58
  57.4 0.1 eq.46
  57.5 0.1 eq.42
  57.6 0.1 copy.60
  57.7 0.3 fusion.5
  58.1 0.1 broadcast_add_fusion
  58.2 0.3 copy.61
  58.5 0.1 copy.57
  58.6 0.1 mul.48
  58.8 0.1 copy.62
  58.9 0.1 reshape.128
  59.0 0.3 fusion.4
  59.3 3.8 scatter_custom_fusion
  63.1 0.3 reshape.109
  63.3 0.8 copy.63
  64.1 18.7 %all-to-all-start = ((bf16[16,32,2]{1,2,0:T(2,128)(2,1)}), bf16[16,32,2]{1,2,0:T(2,128)(2,1)S(1)}, u32[]{:S(2)}, u32[]{:S(2)}) async-start(bf16[16,32,2]{1,2,0:T(2,128)(2,1)} %copy.63), calls=%async_computation | async-start | bytes 16384 | tf_op jit(solution)/shard_map/all_to_all | solution.py:54
  82.9 2.8 scatter_custom_fusion.1
  85.6 4.3 %all-to-all-done = bf16[16,32,2]{1,2,0:T(2,128)(2,1)S(1)} async-done(((bf16[16,32,2]{1,2,0:T(2,128)(2,1)}), bf16[16,32,2]{1,2,0:T(2,128)(2,1)S(1)}, u32[]{:S(2)}, u32[]{:S(2)}) %all-to-all-start) | async-done | bytes 2080 | tf_op jit(solution)/shard_map/all_to_all | solution.py:54
  90.0 3.9 all-to-all-start.2
  93.9 0.7 copy.64
  94.5 13.3 %all-to-all-done.2 = bf16[16,32,2,128]{3,2,1,0:T(2,128)(2,1)S(1)} async-done(((bf16[16,32,2,128]{3,2,1,0:T(2,128)(2,1)}), bf16[16,32,2,128]{3,2,1,0:T(2,128)(2,1)S(1)}, u32[]{:S(2)}, u32[]{:S(2)}) %all-to-all-start.2) | async-done | bytes 262176 | tf_op jit(solution)/shard_map/all_to_all | solution.py:47
  107.9 4.7 %all-to-all-start.1 = ((bf16[16,32,2]{0,2,1:T(2,128)(2,1)}), bf16[16,32,2]{0,2,1:T(2,128)(2,1)S(1)}, u32[]{:S(2)}, u32[]{:S(2)}) async-start(bf16[16,32,2]{0,2,1:T(2,128)(2,1)} %copy.64), calls=%async_computation.1 | async-start | bytes 32768 | tf_op jit(solution)/shard_map/all_to_all | solution.py:53
  112.6 0.9 copy.67
  113.5 7.7 %all-to-all-done.1 = bf16[16,32,2]{0,2,1:T(2,128)(2,1)S(1)} async-done(((bf16[16,32,2]{0,2,1:T(2,128)(2,1)}), bf16[16,32,2]{0,2,1:T(2,128)(2,1)S(1)}, u32[]{:S(2)}, u32[]{:S(2)}) %all-to-all-start.1) | async-done | bytes 2080 | tf_op jit(solution)/shard_map/all_to_all | solution.py:53
  121.2 4.0 all-to-all-start.3
  125.4 0.2 copy.66
  125.6 0.2 reshape.114
  125.7 0.2 fusion.12
  126.0 8.8 %all-to-all-done.3 = bf16[16,32,2,128]{3,2,0,1:T(2,128)(2,1)S(1)} async-done(((bf16[16,32,2,128]{3,2,0,1:T(2,128)(2,1)}), bf16[16,32,2,128]{3,2,0,1:T(2,128)(2,1)S(1)}, u32[]{:S(2)}, u32[]{:S(2)}) %all-to-all-start.3) | async-done | bytes 262176 | tf_op jit(solution)/shard_map/all_to_all | solution.py:46
  134.8 0.2 copy.68
  135.0 3.5 broadcast_multiply_fusion
  138.5 8.3 %convolution_convert_fusion = bf16[1024,2048]{1,0:T(8,128)(2,1)} fusion(bf16[1024,2048]{1,0:T(8,128)(2,1)} %param.14, bf16[128,8,8,128]{3,2,1,0:T(8,128)(2,1)S(1)} %bitcast.26), kind=kOutput, calls=%fused_computation.3 | convolution fusion | flops 4297064448 | bytes 10485760 | tf_op jit(solution)/shard_map/dot_general | solution.py:67
  146.8 7.6 %reshape.112 = bf16[16,32,2,2048]{3,2,1,0:T(2,128)(2,1)} reshape(bf16[1024,2048]{1,0:T(8,128)(2,1)} %convolution_convert_fusion) | data formatting | bytes 8388608 | tf_op jit(solution)/shard_map/reshape | solution.py:70
  154.4 8.1 %all-to-all-start.4 = ((bf16[16,32,2,2048]{3,2,1,0:T(2,128)(2,1)}), bf16[16,32,2,2048]{3,2,1,0:T(2,128)(2,1)}, u32[]{:S(2)}, u32[]{:S(2)}) async-start(bf16[16,32,2,2048]{3,2,1,0:T(2,128)(2,1)} %reshape.112), calls=%async_computation.4 | async-start | bytes 8388608 | tf_op jit(solution)/shard_map/all_to_all | solution.py:72
  162.5 40.7 %all_gather.14 = bf16[96,1536]{0,1:T(8,128)(2,1)S(1)} all-gather(bf16[96,48]{0,1:T(8,128)(2,1)S(1)} %copy-done.1), channel_id=1, replica_groups=mesh['vocab'=16,'docs'=32] {'docs'}, dimensions={1}, use_global_device_ids=true | all-gather | bytes 304128 | tf_op jit(solution)/shard_map/all_gather | solution.py:89
  203.3 0.9 copy.71
  204.2 65.5 %all-to-all-done.4 = bf16[16,32,2,2048]{3,2,1,0:T(2,128)(2,1)} async-done(((bf16[16,32,2,2048]{3,2,1,0:T(2,128)(2,1)}), bf16[16,32,2,2048]{3,2,1,0:T(2,128)(2,1)}, u32[]{:S(2)}, u32[]{:S(2)}) %all-to-all-start.4) | async-done | bytes 4194336 | tf_op jit(solution)/shard_map/all_to_all | solution.py:72
  269.7 8.8 %copy.69 = bf16[16,32,2,2048]{3,2,0,1:T(2,128)(2,1)} copy(bf16[16,32,2,2048]{3,2,1,0:T(2,128)(2,1)} %all-to-all-done.4) | data formatting | bytes 8388608 | tf_op jit(solution)/shard_map/all_to_all | solution.py:72
  278.5 5.2 %all-to-all-start.5 = ((bf16[16,32,2,2048]{3,2,0,1:T(2,128)(2,1)}), bf16[16,32,2,2048]{3,2,0,1:T(2,128)(2,1)}, u32[]{:S(2)}, u32[]{:S(2)}) async-start(bf16[16,32,2,2048]{3,2,0,1:T(2,128)(2,1)} %copy.69), calls=%async_computation.5 | async-start | bytes 8388608 | tf_op jit(solution)/shard_map/all_to_all | solution.py:71
  283.8 94.4 %all-to-all-done.5 = bf16[16,32,2,2048]{3,2,0,1:T(2,128)(2,1)} async-done(((bf16[16,32,2,2048]{3,2,0,1:T(2,128)(2,1)}), bf16[16,32,2,2048]{3,2,0,1:T(2,128)(2,1)}, u32[]{:S(2)}, u32[]{:S(2)}) %all-to-all-start.5) | async-done | bytes 4194336 | tf_op jit(solution)/shard_map/all_to_all | solution.py:71
  378.2 8.0 %copy.70 = bf16[16,32,2,2048]{3,2,1,0:T(2,128)(2,1)} copy(bf16[16,32,2,2048]{3,2,0,1:T(2,128)(2,1)} %all-to-all-done.5) | data formatting | bytes 8388608 | tf_op jit(solution)/shard_map/all_to_all | solution.py:71
  386.2 7.2 %reshape.113 = bf16[1024,2048]{1,0:T(8,128)(2,1)} reshape(bf16[16,32,2,2048]{3,2,1,0:T(2,128)(2,1)} %copy.70) | data formatting | bytes 8388608 | tf_op jit(solution)/shard_map/reshape | solution.py:78
  393.4 7.1 %gather_fusion = bf16[512,2048]{1,0:T(8,128)(2,1)S(1)} fusion(bf16[1024,2048]{1,0:T(8,128)(2,1)} %reshape.113, s32[1024]{0:T(1024)S(1)} %pad_clamp_fusion), kind=kCustom, calls=%fused_computation | custom fusion | bytes 4196352 | tf_op jit(solution)/shard_map/gather | solution.py:79
  400.6 3.0 reshape.115
  403.6 4.8 %reduce_sum.19 = f32[128,2048]{1,0:T(8,128)S(1)} reduce(f32[128,4,2048]{2,1,0:T(4,128)} %reshape.115, f32[]{:T(128)} %constant.6.clone.1), dimensions={1}, to_apply=%region_5.6 | reduce | flops 786432 | bytes 5242884 | tf_op jit(solution)/shard_map/reduce_sum | solution.py:80
  408.5 5.1 %convolution_add_fusion.1 = f32[128,1536]{1,0:T(8,128)S(1)} fusion(bf16[2048,1536]{0,1:T(8,128)(2,1)} %all-gather.3.cloned.1.call-done, f32[128,2048]{1,0:T(8,128)S(1)} %reduce_sum.19, f32[2048]{0:T(1024)S(1)} %copy-done.4, f32[128]{0:T(128)S(1)} %convert_divide_fusion, f32[1536]{0:T(1024)S(1)} %copy-done.5), kind=kOutput, calls=%fused_computation.6 | convolution fusion | flops 807862272 | bytes 8141312 | tf_op jit(solution)/shard_map/dot_general | solution.py:84
  413.7 4.7 %fusion = bf16[128,1536]{1,0:T(8,128)(2,1)} fusion(f32[128,1536]{1,0:T(8,128)S(1)} %convolution_add_fusion.1, bf16[128,1536]{1,0:T(8,128)(2,1)S(1)} %copy-done, bf16[1536,1536]{1,0:T(8,128)(2,1)} %all-gather.5.cloned.1.call-done), kind=kOutput, calls=%fused_computation.7 | convolution fusion | flops 604372992 | bytes 6291456 | tf_op jit(solution)/shard_map/dot_general | solution.py:90
  (32 shorter events, 0.3 us)
Async XLA Ops:
  6.5 407.1 %copy-start = (bf16[128,1536]{1,0:T(8,128)(2,1)S(1)}, bf16[128,1536]{1,0:T(8,128)(2,1)}, u32[]{:S(2)}) copy-start(bf16[128,1536]{1,0:T(8,128)(2,1)} %param.19) | copy-start | bytes 1179652
  6.5 52.0 %copy-start.2 = (s32[128,4]{0,1:T(4,128)S(1)}, s32[128,4]{0,1:T(4,128)}, u32[]{:S(2)}) copy-start(s32[128,4]{0,1:T(4,128)} %param.11) | copy-start | bytes 6148
  6.5 52.2 %copy-start.3 = (s32[128,4]{0,1:T(4,128)S(1)}, s32[128,4]{0,1:T(4,128)}, u32[]{:S(2)}) copy-start(s32[128,4]{0,1:T(4,128)} %param.12) | copy-start | bytes 6148
  6.5 402.0 %all-gather.3.cloned.1.call-start = ((), (), s32[]{:S(2)}) async-start(), calls=%async_computation.6 | async-start | bytes 6684672 | tf_op jit(solution)/shard_map/all_gather | solution.py:86
  64.1 25.8 %all-to-all-start = ((bf16[16,32,2]{1,2,0:T(2,128)(2,1)}), bf16[16,32,2]{1,2,0:T(2,128)(2,1)S(1)}, u32[]{:S(2)}, u32[]{:S(2)}) async-start(bf16[16,32,2]{1,2,0:T(2,128)(2,1)} %copy.63), calls=%async_computation | async-start | bytes 16384 | tf_op jit(solution)/shard_map/all_to_all | solution.py:54
  90.0 17.9 %all-to-all-start.2 = ((bf16[16,32,2,128]{3,2,1,0:T(2,128)(2,1)}), bf16[16,32,2,128]{3,2,1,0:T(2,128)(2,1)S(1)}, u32[]{:S(2)}, u32[]{:S(2)}) async-start(bf16[16,32,2,128]{3,2,1,0:T(2,128)(2,1)} %bitcast.6), calls=%async_computation.2 | async-start | bytes 524288 | tf_op jit(solution)/shard_map/all_to_all | solution.py:47
  107.9 13.3 %all-to-all-start.1 = ((bf16[16,32,2]{0,2,1:T(2,128)(2,1)}), bf16[16,32,2]{0,2,1:T(2,128)(2,1)S(1)}, u32[]{:S(2)}, u32[]{:S(2)}) async-start(bf16[16,32,2]{0,2,1:T(2,128)(2,1)} %copy.64), calls=%async_computation.1 | async-start | bytes 32768 | tf_op jit(solution)/shard_map/all_to_all | solution.py:53
  121.2 13.5 %all-to-all-start.3 = ((bf16[16,32,2,128]{3,2,0,1:T(2,128)(2,1)}), bf16[16,32,2,128]{3,2,0,1:T(2,128)(2,1)S(1)}, u32[]{:S(2)}, u32[]{:S(2)}) async-start(bf16[16,32,2,128]{3,2,0,1:T(2,128)(2,1)} %copy.67), calls=%async_computation.3 | async-start | bytes 524288 | tf_op jit(solution)/shard_map/all_to_all | solution.py:46
  154.4 8.1 %copy-start.1 = (bf16[96,48]{0,1:T(8,128)(2,1)S(1)}, bf16[96,48]{0,1:T(8,128)(2,1)}, u32[]{:S(2)}) copy-start(bf16[96,48]{0,1:T(8,128)(2,1)} %param.18) | copy-start | bytes 27652
  154.4 115.3 %all-to-all-start.4 = ((bf16[16,32,2,2048]{3,2,1,0:T(2,128)(2,1)}), bf16[16,32,2,2048]{3,2,1,0:T(2,128)(2,1)}, u32[]{:S(2)}, u32[]{:S(2)}) async-start(bf16[16,32,2,2048]{3,2,1,0:T(2,128)(2,1)} %reshape.112), calls=%async_computation.4 | async-start | bytes 8388608 | tf_op jit(solution)/shard_map/all_to_all | solution.py:72
  162.5 251.2 %all-gather.5.cloned.1.call-start = ((), (), s32[]{:S(2)}) async-start(), calls=%async_computation.7 | async-start | bytes 5013504 | tf_op jit(solution)/shard_map/all_gather | solution.py:92
  278.5 5.2 %copy-start.6 = (s32[128]{0:T(128)S(1)}, s32[128]{0:T(128)}, u32[]{:S(2)}) copy-start(s32[128]{0:T(128)} %param.13) | copy-start | bytes 1540
  278.5 99.7 %all-to-all-start.5 = ((bf16[16,32,2,2048]{3,2,0,1:T(2,128)(2,1)}), bf16[16,32,2,2048]{3,2,0,1:T(2,128)(2,1)}, u32[]{:S(2)}, u32[]{:S(2)}) async-start(bf16[16,32,2,2048]{3,2,0,1:T(2,128)(2,1)} %copy.69), calls=%async_computation.5 | async-start | bytes 8388608 | tf_op jit(solution)/shard_map/all_to_all | solution.py:71
  403.6 4.9 %copy-start.4 = (f32[2048]{0:T(1024)S(1)}, f32[2048]{0:T(1024)}, u32[]{:S(2)}) copy-start(f32[2048]{0:T(1024)} %param.15) | copy-start | bytes 24580
  403.6 4.9 %copy-start.5 = (f32[1536]{0:T(1024)S(1)}, f32[1536]{0:T(1024)}, u32[]{:S(2)}) copy-start(f32[1536]{0:T(1024)} %param.17) | copy-start | bytes 18436
Sparse Core Ops, SparseCore 0:
  56.7 72.7 all-gather.2
  204.3 78.6 all-gather.4
where the time goes:
time: 426 us; the launch traced here: 425 us
  waiting for transfers between devices  194 us (46%)
  blocking collectives  90.8 us (21%)
  local copies, waits for them, and re-layouts  54.5 us (13%)
  starting transfers between devices  44.7 us (10%)
  matrix products  18.1 us (4%)
  between operations  13.7 us (3%)
  other arithmetic  9.24 us (2%)
    all_to_all x1, waiting for transfers between devices, local(): lax.all_to_all(lax.all_to_all(owner_terms, 'vocab', split_axis=0, concat_...  94.4 us
    all_to_all x1, waiting for transfers between devices, local(): lax.all_to_all(owner_terms, 'vocab', split_axis=0, concat_axis=0, tiled=T...  65.5 us
    all_gather x1, blocking collectives, local(): panel_rows = lax.all_gather(head_weight, 'docs', axis=1, tiled=True)  50 us
    all_gather x1, blocking collectives, local(): factor_panel = lax.all_gather(factor, 'docs', axis=1, tiled=True)  40.7 us
    all_to_all x1, starting transfers between devices, local(): lax.all_to_all(send_sub, 'vocab', split_axis=0, concat_axis=0, tiled=True)  18.7 us
    all_to_all x1, waiting for transfers between devices, local(): lax.all_to_all(send_rows, 'vocab', split_axis=0, concat_axis=0, tiled=True)  13.3 us
    all_to_all x1, waiting for transfers between devices, local(): lax.all_to_all(lax.all_to_all(send_rows, 'vocab', split_axis=0, concat_ax...  8.81 us
    all_to_all x1, local copies, waits for them, and re-layouts, local(): lax.all_to_all(owner_terms, 'vocab', split_axis=0, concat_axis=0, tiled=T...  8.8 us
  transfers between devices with their start and end apart: 8, of which 6 were waited for; matrix products, arithmetic and copies ran while one was open for 18% of the time, Pallas kernels for 0%

commit v1 on v0

v1 whole, which is shorter than its diff:
```python
import functools

import jax
import jax.numpy as jnp
from jax import lax
from jax.experimental import pallas as pl
from jax.experimental.pallas import tpu as pltpu
from jax.sharding import PartitionSpec as P

AXES = ("vocab", "docs")
VMEM = pl.BlockSpec(memory_space=pltpu.VMEM)
SMEM = pl.BlockSpec(memory_space=pltpu.SMEM)
LANES = 128
PARAMS = pltpu.CompilerParams(vmem_limit_bytes=56 * 1024 * 1024)
NT = (((1,), (1,)), ((), ()))


def route_kernel(owner_ref, sub_ref, rows_ref, send_ref, place_ref):
    slots = owner_ref.shape[1]
    devices = send_ref.shape[0]
    owner = owner_ref[...]
    named = owner == lax.broadcasted_iota(jnp.int32, (devices, slots), 0)
    named_b = jnp.where(named, 1.0, 0.0).astype(jnp.bfloat16)
    earlier = lax.broadcasted_iota(jnp.int32, (slots, slots), 0) < lax.broadcasted_iota(
        jnp.int32, (slots, slots), 1
    )
    before = jnp.dot(
        named_b,
        jnp.where(earlier, 1.0, 0.0).astype(jnp.bfloat16),
        preferred_element_type=jnp.float32,
    )
    second = jnp.where(named & (before > 0.5), 1.0, 0.0)
    position = jnp.max(second, axis=0, keepdims=True)
    place_ref[...] = owner * 2 + position.astype(jnp.int32)
    rows = rows_ref[...]
    sub = jnp.broadcast_to(sub_ref[...].astype(jnp.float32), (LANES, slots)).astype(jnp.bfloat16)
    picks = (jnp.where(named & (before < 0.5), 1.0, 0.0).astype(jnp.bfloat16), second.astype(jnp.bfloat16))
    for p, pick in enumerate(picks):
        send_ref[:, p * LANES : (p + 1) * LANES] = jnp.dot(
            pick, rows, preferred_element_type=jnp.float32
        ).astype(jnp.bfloat16)
        send_ref[:, (2 + p) * LANES : (3 + p) * LANES] = lax.dot_general(
            pick, sub, NT, preferred_element_type=jnp.float32
        ).astype(jnp.bfloat16)


def owner_kernel(got_ref, weight_ref, out_ref, spread, stage):
    devices = got_ref.shape[0]
    blocks = weight_ref.shape[0] // LANES
    hidden_width = weight_ref.shape[1]
    for p in range(2):
        rows = got_ref[:, p * LANES : (p + 1) * LANES]
        sub = got_ref[:, (2 + p) * LANES : (3 + p) * LANES].astype(jnp.float32)
        for b in range(blocks):
            spread[p * devices : (p + 1) * devices, b * LANES : (b + 1) * LANES] = jnp.where(
                sub == float(b), rows.astype(jnp.float32), 0.0
            ).astype(jnp.bfloat16)
    width = 256
    parts = hidden_width // LANES
    for g in range(parts // 8):
        for cc in range(8 * LANES // width):
            column = g * 8 * LANES + cc * width
            terms = jnp.dot(
                spread[...], weight_ref[:, column : column + width], preferred_element_type=jnp.float32
            )
            for p in range(2):
                for k in range(width // LANES):
                    c = cc * (width // LANES) + k
                    stage[p, pl.ds(c, devices, stride=8), :] = terms[
                        p * devices : (p + 1) * devices, k * LANES : (k + 1) * LANES
                    ]
        for p in range(2):
            out_ref[:, p * parts + 8 * g : p * parts + 8 * g + 8, :] = (
                stage[p].reshape(devices, 8, LANES).astype(jnp.bfloat16)
            )


def finish_kernel(place_ref, got_ref, scale_ref, bias_ref, head_ref, extra_ref, out_ref, total, head, sem):
    docs, topics = out_ref.shape
    parts = got_ref.shape[1]
    copy = pltpu.make_async_copy(head_ref.at[:, :, pl.ds(0, LANES)], head, sem)
    copy.start()

    @pl.loop(0, docs, unroll=4)
    def _(n):
        value = got_ref[place_ref[0, n]].astype(jnp.float32)
        for slot in range(1, 4):
            value += got_ref[place_ref[0, slot * docs + n]].astype(jnp.float32)
        total[pl.ds(n * parts, parts), :] = value

    copy.wait()
    scale = scale_ref[...]
    result = extra_ref[...]
    for c in range(0, parts, 2):
        pair, columns = [], []
        for k in (c, c + 1):
            v = total[pl.ds(k, docs, stride=parts), :] * scale + bias_ref[:, k * LANES : (k + 1) * LANES]
            pair.append(jnp.maximum(v, 0.0) + jnp.log1p(jnp.exp(-jnp.abs(v))))
            columns.append(head[k])
        hidden = jnp.concatenate(pair, axis=1).astype(jnp.bfloat16)
        result += lax.dot_general(
            hidden, jnp.concatenate(columns, axis=1), NT, preferred_element_type=jnp.float32
        )
    out_ref[...] = result.astype(jnp.bfloat16)


def local(
    counts,
    doc_owner,
    doc_sub,
    doc_len,
    first_weight,
    first_bias,
    head_weight,
    head_bias,
    factor,
    noise_draw,
):
    vocab_devices = lax.axis_size("vocab")
    docs_devices = lax.axis_size("docs")
    devices = vocab_devices * docs_devices
    docs_here, slot_count, block_width = counts.shape
    slots = docs_here * slot_count
    hidden_width = first_weight.shape[1]
    parts = hidden_width // LANES
    topics = noise_draw.shape[1]
    topic_cols = head_weight.shape[1]
    factor_rows = factor.shape[0]

    panel = jnp.concatenate(
        [head_weight.T, jnp.pad(factor.T, ((0, 0), (0, LANES - factor_rows)))], axis=1
    )
    panels = lax.all_gather(panel, AXES, axis=0, tiled=True)
    panels = panels.reshape(vocab_devices, docs_devices * topic_cols, 2 * LANES)

    rows = counts.transpose(1, 0, 2).reshape(slots, block_width)
    owner_flat = doc_owner.T.reshape(1, slots)
    sub_flat = doc_sub.T.reshape(1, slots)
    send, place = pl.pallas_call(
        route_kernel,
        out_shape=(
            jax.ShapeDtypeStruct((devices, 4 * LANES), jnp.bfloat16),
            jax.ShapeDtypeStruct((1, slots), jnp.int32),
        ),
        in_specs=[VMEM] * 3,
        out_specs=(VMEM, VMEM),
        compiler_params=PARAMS,
        cost_estimate=pl.CostEstimate(flops=10**9, bytes_accessed=10**6, transcendentals=0),
    )(owner_flat, sub_flat, rows)
    got = lax.all_to_all(
        send.reshape(devices, 4, LANES), AXES, split_axis=0, concat_axis=0, tiled=True
    )
    terms = pl.pallas_call(
        owner_kernel,
        out_shape=jax.ShapeDtypeStruct((devices, 2 * parts, LANES), jnp.bfloat16),
        in_specs=[VMEM] * 2,
        out_specs=VMEM,
        scratch_shapes=[
            pltpu.VMEM((2 * devices, first_weight.shape[0]), jnp.bfloat16),
            pltpu.VMEM((2, devices * 8, LANES), jnp.float32),
        ],
        compiler_params=PARAMS,
        cost_estimate=pl.CostEstimate(flops=5 * 10**9, bytes_accessed=10**7, transcendentals=0),
    )(got.reshape(devices, 4 * LANES), first_weight)
    returned = lax.all_to_all(terms, AXES, split_axis=0, concat_axis=0, tiled=True)
    returned = returned.reshape(2 * devices, parts, LANES)

    correlated = jnp.einsum(
        "nj,vjk->nvk",
        noise_draw,
        panels[:, :, LANES : LANES + factor_rows],
        preferred_element_type=jnp.float32,
    ).reshape(docs_here, topics)
    extra = correlated + head_bias
    scale = (128.0 * slot_count / doc_len.astype(jnp.float32))[:, None]
    return pl.pallas_call(
        finish_kernel,
        out_shape=jax.ShapeDtypeStruct((docs_here, topics), jnp.bfloat16),
        in_specs=[SMEM, VMEM, VMEM, VMEM, pl.BlockSpec(memory_space=pl.ANY), VMEM],
        out_specs=VMEM,
        scratch_shapes=[
            pltpu.VMEM((docs_here * parts, LANES), jnp.float32),
            pltpu.VMEM((vocab_devices, topics, LANES), jnp.bfloat16),
            pltpu.SemaphoreType.DMA,
        ],
        compiler_params=PARAMS,
        cost_estimate=pl.CostEstimate(flops=10**9, bytes_accessed=10**7, transcendentals=10**6),
    )(place, returned, scale, first_bias.reshape(1, hidden_width), panels, extra)


def solution(mesh):
    return jax.shard_map(
        local,
        mesh=mesh,
        in_specs=(
            P(("vocab", "docs"), None, None),
            P(("vocab", "docs"), None),
            P(("vocab", "docs"), None),
            P(("vocab", "docs")),
            P(("vocab", "docs"), None),
            P(),
            P("vocab", "docs"),
            P(),
            P("vocab", "docs"),
            P(("vocab", "docs"), None),
        ),
        out_specs=P(("vocab", "docs"), None),
        check_vma=False,
    )
```

time: 426 us -> 246 us (0.58)
  waiting for transfers between devices: 194 us -> 143 us
  local copies, waits for them, and re-layouts: 54.5 us -> 4.67 us
  blocking collectives: 90.8 us -> 43.7 us
  starting transfers between devices: 44.7 us -> 12.9 us
  Pallas kernels: 0 us -> 20.7 us
  matrix products: 18.1 us -> 4.6 us
  other arithmetic: 9.24 us -> 2.35 us
    all_to_all x6 -> x1, waiting for transfers between devices: 194 us -> 0.01 us  [local(): lax.all_to_all(terms, AXES, split_axis=0, concat_axis=0, tiled=True)]
    all_gather x2 -> x1, waiting for transfers between devices: 0.04 us -> 143 us  [local(): panels = lax.all_gather(panel, AXES, axis=0, tiled=True)]
    all_gather x2 -> x0, blocking collectives: 90.8 us -> none  [the longest x1 50 us: local(): panel_rows = lax.all_gather(head_weight, 'docs', axis=1, tiled=True)]
    all_to_all x0 -> x1, blocking collectives: none -> 43.7 us  [local(): lax.all_to_all(send.reshape(devices, 4, LANES), AXES, split_axis=0, conca...]
    all_to_all x6 -> x1, starting transfers between devices: 44.7 us -> 12.9 us  [local(): lax.all_to_all(terms, AXES, split_axis=0, concat_axis=0, tiled=True)]
    pallas_call x0 -> x3, Pallas kernels: none -> 20.7 us  [the longest x1 9.72 us: local(): pl.pallas_call(owner_kernel, out_shape=jax.ShapeDtypeStruct((devices, 2 *...]
    all_to_all x6 -> x0, local copies, waits for them, and re-layouts: 18.7 us -> none  [the longest x1 8.8 us: local(): lax.all_to_all(owner_terms, 'vocab', split_axis=0, concat_axis=0, tiled=T...]
    reshape x4 -> x2, local copies, waits for them, and re-layouts: 15.8 us -> 1.43 us  [the longest x1 1.16 us: local(): send.reshape(devices, 4, LANES)]
  transfers between devices with their start and end apart: 8 -> 2, of which waited for: 6 -> 1; matrix products, arithmetic and copies ran while one was open for 18% -> 4% of each run, Pallas kernels for 0% -> 5%
where the time goes in v1:
time: 246 us
  waiting for transfers between devices  143 us (58%)
  blocking collectives  43.7 us (18%)
  Pallas kernels  20.7 us (8%)
  between operations  13.5 us (5%)
  starting transfers between devices  12.9 us (5%)
  local copies, waits for them, and re-layouts  4.67 us (2%)
  matrix products  4.6 us (2%)
    all_gather x1, waiting for transfers between devices, local(): panels = lax.all_gather(panel, AXES, axis=0, tiled=True)  143 us
    all_to_all x1, blocking collectives, local(): lax.all_to_all(send.reshape(devices, 4, LANES), AXES, split_axis=0, conca...  43.7 us
    all_to_all x1, starting transfers between devices, local(): lax.all_to_all(terms, AXES, split_axis=0, concat_axis=0, tiled=True)  12.9 us
    pallas_call x1, Pallas kernels, local(): pl.pallas_call(owner_kernel, out_shape=jax.ShapeDtypeStruct((devices, 2 *...  9.72 us
    pallas_call x1, Pallas kernels, local(): pl.pallas_call(finish_kernel, out_shape=jax.ShapeDtypeStruct((docs_here,...  8.22 us
  transfers between devices with their start and end apart: 2, of which 1 were waited for; matrix products, arithmetic and copies ran while one was open for 4% of the time, Pallas kernels for 5%

profile of v1, /device:TPU:1, one launch (start us, length us, event | category | flops | bytes accessed | tf_op | source)
XLA Modules:
  0.0 245.6 jit_solution(12733871456131341097)
XLA Ops:
  6.5 0.0 copy-start
  6.5 0.0 all-gather.2.cloned.1.call-start
  6.5 1.4 fusion.4
  7.9 0.0 all-gather.2.cloned.1.call-update
  7.9 1.6 copy.15
  9.5 2.8 %shard_map.100 = (bf16[512,512]{1,0:T(8,128)(2,1)}, s32[1,512]{1,0:T(1,128)}) custom-call(s32[1,512]{1,0:T(1,128)} %bitcast.35, s32[1,512]{1,0:T(1,128)} %bitcast.36, bf16[512,128]{1,0:T(8,128)(2,1)} %bitcast.31), custom_call_target="tpu_custom_call" | custom-call | flops 1000000000 | bytes 1000000 | tf_op jit(solution)/shard_map/pallas_call | solution.py:139
  12.3 1.2 reshape.31
  13.5 43.7 %all_to_all.10 = bf16[512,4,128]{2,1,0:T(4,128)(2,1)S(1)} all-to-all(bf16[512,4,128]{2,1,0:T(4,128)(2,1)S(1)} %reshape.31), channel_id=1, replica_groups=mesh['vocab'=16,'docs'=32] {'vocab','docs'}, dimensions={0} | all-to-all | bytes 1048576 | tf_op jit(solution)/shard_map/all_to_all | solution.py:150
  57.2 0.9 copy.22
  58.1 9.7 %shard_map.101 = bf16[512,32,128]{2,1,0:T(8,128)(2,1)} custom-call(bf16[512,512]{1,0:T(8,128)(2,1)} %bitcast.29, bf16[1024,2048]{1,0:T(8,128)(2,1)} %weight_ref.1), custom_call_target="tpu_custom_call" | custom-call | flops 5000000000 | bytes 10000000 | tf_op jit(solution)/shard_map/pallas_call | solution.py:153
  67.8 0.0 copy-start.2
  67.9 12.9 %all-to-all-start.1 = ((bf16[512,32,128]{2,1,0:T(8,128)(2,1)}), bf16[512,32,128]{2,1,0:T(8,128)(2,1)}, u32[]{:S(2)}, u32[]{:S(2)}) async-start(bf16[512,32,128]{2,1,0:T(8,128)(2,1)} %shard_map.101), calls=%async_computation.1 | async-start | bytes 8388608 | tf_op jit(solution)/shard_map/all_to_all | solution.py:165
  80.8 0.0 copy-done.2
  80.8 0.0 copy-start.1
  80.8 0.7 copy.18.scale_ref
  81.5 143.1 %all-gather.2.cloned.1.call-done = bf16[24576,256]{1,0:T(8,128)(2,1)} async-done(((bf16[48,256]{1,0:T(8,128)(2,1)}), bf16[24576,256]{1,0:T(8,128)(2,1)}) %all-gather.2.cloned.1.call-update) | async-done | bytes 12582928 | tf_op jit(solution)/shard_map/all_gather | solution.py:133
  224.7 0.0 copy-done
  224.7 4.6 %fusion = f32[16,96,128]{2,1,0:T(8,128)S(1)} fusion(bf16[16,1536,256]{2,1,0:T(8,128)(2,1)} %bitcast.25, bf16[128,1536]{1,0:T(8,128)(2,1)S(1)} %copy-done), kind=kOutput, calls=%fused_computation | convolution fusion | flops 603979776 | bytes 7471104 | tf_op jit(solution)/shard_map/nj,vjk->nvk/dot_general | solution.py:168
  229.3 0.3 copy.17
  229.5 0.0 copy-done.1
  229.5 1.0 broadcast_add_fusion.extra_ref
  230.5 0.0 all-to-all-done.1
  230.5 8.2 %shard_map.102 = bf16[128,1536]{1,0:T(8,128)(2,1)} custom-call(s32[1,512]{1,0:T(1,128)} %get-tuple-element.7.place_ref, bf16[1024,16,128]{2,1,0:T(8,128)(2,1)} %bitcast.6.got_ref, f32[128,1]{1,0:T(8,128)} %copy.18.scale_ref, f32[1,2048]{1,0:T(1,128)} %bitcast.34, bf16[16,1536,256]{2,1,0:T(8,128)(2,1)} %bitcast.26, f32[128,1536]{1,0:T(8,128)} %broadcast_add_fusion.extra_ref), custom_call_target="tpu_custom_call" | custom-call | flops 1000000000 | bytes 10000000 | tf_op jit(solution)/shard_map/pallas_call | solution.py:176
  (1 shorter events, 0.0 us)
Async XLA Ops:
  6.5 218.1 %copy-start = (bf16[128,1536]{1,0:T(8,128)(2,1)S(1)}, bf16[128,1536]{1,0:T(8,128)(2,1)}, u32[]{:S(2)}) copy-start(bf16[128,1536]{1,0:T(8,128)(2,1)} %param.19) | copy-start | bytes 1179652
  6.5 218.1 %all-gather.2.cloned.1.call-start = ((), (), s32[]{:S(2)}) async-start(), calls=%async_computation.2 | async-start | bytes 12607488 | tf_op jit(solution)/shard_map/all_gather | solution.py:133
  67.8 12.9 %copy-start.2 = (s32[128]{0:T(128)S(1)}, s32[128]{0:T(128)}, u32[]{:S(2)}) copy-start(s32[128]{0:T(128)} %param.13) | copy-start | bytes 1540
  67.9 162.7 %all-to-all-start.1 = ((bf16[512,32,128]{2,1,0:T(8,128)(2,1)}), bf16[512,32,128]{2,1,0:T(8,128)(2,1)}, u32[]{:S(2)}, u32[]{:S(2)}) async-start(bf16[512,32,128]{2,1,0:T(8,128)(2,1)} %shard_map.101), calls=%async_computation.1 | async-start | bytes 8388608 | tf_op jit(solution)/shard_map/all_to_all | solution.py:165
  80.8 148.8 %copy-start.1 = (f32[1536]{0:T(1024)S(1)}, f32[1536]{0:T(1024)}, u32[]{:S(2)}) copy-start(f32[1536]{0:T(1024)} %param.17) | copy-start | bytes 18436
Sparse Core Ops, SparseCore 0:
  12.1 212.5 all-gather.1

commit v2 on v1

--- a/solution.py
+++ b/solution.py
@@ -1,5 +1,3 @@
-import functools
-
 import jax
 import jax.numpy as jnp
 from jax import lax
@@ -7,7 +5,7 @@
 from jax.experimental.pallas import tpu as pltpu
 from jax.sharding import PartitionSpec as P
 
-AXES = ("vocab", "docs")
+AXES = ("y", "core", "x", "z")
 VMEM = pl.BlockSpec(memory_space=pltpu.VMEM)
 SMEM = pl.BlockSpec(memory_space=pltpu.SMEM)
 LANES = 128
@@ -47,7 +45,7 @@
 def owner_kernel(got_ref, weight_ref, out_ref, spread, stage):
     devices = got_ref.shape[0]
     blocks = weight_ref.shape[0] // LANES
-    hidden_width = weight_ref.shape[1]
+    parts = weight_ref.shape[1] // LANES
     for p in range(2):
         rows = got_ref[:, p * LANES : (p + 1) * LANES]
         sub = got_ref[:, (2 + p) * LANES : (3 + p) * LANES].astype(jnp.float32)
@@ -56,7 +54,6 @@
                 sub == float(b), rows.astype(jnp.float32), 0.0
             ).astype(jnp.bfloat16)
     width = 256
-    parts = hidden_width // LANES
     for g in range(parts // 8):
         for cc in range(8 * LANES // width):
             column = g * 8 * LANES + cc * width
@@ -75,33 +72,66 @@
             )
 
 
-def finish_kernel(place_ref, got_ref, scale_ref, bias_ref, head_ref, extra_ref, out_ref, total, head, sem):
-    docs, topics = out_ref.shape
+def place_panels(shift_ref, panels_ref, lane, target, sem):
+    z_devices, x_devices, rows = panels_ref.shape[1], panels_ref.shape[2], panels_ref.shape[3]
+    copies = []
+    for z in range(z_devices):
+        for k in range(x_devices):
+            x = lax.rem(shift_ref[0] + k, x_devices)
+            begin = pl.multiple_of((x * z_devices + z) * rows, 16)
+            copies.append(
+                pltpu.make_async_copy(
+                    panels_ref.at[:, z, k, :, pl.ds(lane, LANES)],
+                    target.at[:, pl.ds(begin, rows), :],
+                    sem.at[z * x_devices + k],
+                )
+            )
+    for copy in copies:
+        copy.start()
+    return copies
+
+
+def hidden_kernel(place_ref, got_ref, scale_ref, bias_ref, out_ref, total):
+    docs = out_ref.shape[0]
     parts = got_ref.shape[1]
-    copy = pltpu.make_async_copy(head_ref.at[:, :, pl.ds(0, LANES)], head, sem)
-    copy.start()
 
     @pl.loop(0, docs, unroll=4)
     def _(n):
-        value = got_ref[place_ref[0, n]].astype(jnp.float32)
-        for slot in range(1, 4):
-            value += got_ref[place_ref[0, slot * docs + n]].astype(jnp.float32)
-        total[pl.ds(n * parts, parts), :] = value
-
-    copy.wait()
+        value = None
+        for slot in range(4):
+            row = got_ref[place_ref[0, slot * docs + n]].astype(jnp.float32)
+            value = row if value is None else value + row
+        total[pl.ds(pl.multiple_of(n * parts, parts), parts), :] = value
+
     scale = scale_ref[...]
-    result = extra_ref[...]
-    for c in range(0, parts, 2):
-        pair, columns = [], []
-        for k in (c, c + 1):
-            v = total[pl.ds(k, docs, stride=parts), :] * scale + bias_ref[:, k * LANES : (k + 1) * LANES]
-            pair.append(jnp.maximum(v, 0.0) + jnp.log1p(jnp.exp(-jnp.abs(v))))
-            columns.append(head[k])
-        hidden = jnp.concatenate(pair, axis=1).astype(jnp.bfloat16)
-        result += lax.dot_general(
-            hidden, jnp.concatenate(columns, axis=1), NT, preferred_element_type=jnp.float32
-        )
-    out_ref[...] = result.astype(jnp.bfloat16)
+    for c in range(parts):
+        lanes = slice(c * LANES, (c + 1) * LANES)
+        v = total[pl.ds(c, docs, stride=parts), :] * scale + bias_ref[:, lanes]
+        soft = jnp.maximum(v, 0.0) + jnp.log1p(jnp.exp(-jnp.abs(v)))
+        out_ref[:, lanes] = soft.astype(jnp.bfloat16)
+
+
+def output_kernel(shift_ref, hidden_ref, noise_ref, panels_ref, bias_ref, out_ref, head, factor, head_sem, factor_sem):
+    head_copies = place_panels(shift_ref, panels_ref, 0, head, head_sem)
+    factor_copies = place_panels(shift_ref, panels_ref, LANES, factor, factor_sem)
+    pieces = head.shape[0]
+    width = out_ref.shape[1] // pieces
+    for copy in head_copies:
+        copy.wait()
+    result = bias_ref[...]
+    for v in range(0, pieces, 2):
+        hidden = hidden_ref[:, v * LANES : (v + 2) * LANES]
+        pair = jnp.concatenate([head[v], head[v + 1]], axis=1)
+        result = result + lax.dot_general(hidden, pair, NT, preferred_element_type=jnp.float32)
+    for copy in factor_copies:
+        copy.wait()
+    noise = noise_ref[...]
+    parts = []
+    for v in range(0, pieces, 2):
+        pair = jnp.concatenate([factor[v], factor[v + 1]], axis=1)
+        both = jnp.dot(noise, pair, preferred_element_type=jnp.float32)
+        parts += [both[:, :width], both[:, LANES : LANES + width]]
+    out_ref[...] = (result + jnp.concatenate(parts, axis=1)).astype(out_ref.dtype)
 
 
 def local(
@@ -116,8 +146,9 @@
     factor,
     noise_draw,
 ):
-    vocab_devices = lax.axis_size("vocab")
-    docs_devices = lax.axis_size("docs")
+    vocab_devices = lax.axis_size("y") * lax.axis_size("core")
+    x_devices, z_devices = lax.axis_size("x"), lax.axis_size("z")
+    docs_devices = x_devices * z_devices
     devices = vocab_devices * docs_devices
     docs_here, slot_count, block_width = counts.shape
     slots = docs_here * slot_count
@@ -130,9 +161,9 @@
     panel = jnp.concatenate(
         [head_weight.T, jnp.pad(factor.T, ((0, 0), (0, LANES - factor_rows)))], axis=1
     )
-    panels = lax.all_gather(panel, AXES, axis=0, tiled=True)
-    panels = panels.reshape(vocab_devices, docs_devices * topic_cols, 2 * LANES)
-
+    line = [panel]
+    for k in range(1, x_devices):
+        line.append(lax.ppermute(panel, "x", [((i + k) % x_devices, i) for i in range(x_devices)]))
     rows = counts.transpose(1, 0, 2).reshape(slots, block_width)
     owner_flat = doc_owner.T.reshape(1, slots)
     sub_flat = doc_sub.T.reshape(1, slots)
@@ -147,9 +178,15 @@
         compiler_params=PARAMS,
         cost_estimate=pl.CostEstimate(flops=10**9, bytes_accessed=10**6, transcendentals=0),
     )(owner_flat, sub_flat, rows)
+    line, send = lax.optimization_barrier((line, send))
+    panels = lax.all_gather(jnp.concatenate(line, axis=0), ("y", "core", "z"), axis=0, tiled=True)
+    panels = panels.reshape(vocab_devices, z_devices, x_devices, topic_cols, 2 * LANES)
+    shift = lax.axis_index("x").astype(jnp.int32).reshape(1)
+
     got = lax.all_to_all(
         send.reshape(devices, 4, LANES), AXES, split_axis=0, concat_axis=0, tiled=True
     )
+    got = got.reshape(devices, 4 * LANES)
     terms = pl.pallas_call(
         owner_kernel,
         out_shape=jax.ShapeDtypeStruct((devices, 2 * parts, LANES), jnp.bfloat16),
@@ -161,49 +198,44 @@
         ],
         compiler_params=PARAMS,
         cost_estimate=pl.CostEstimate(flops=5 * 10**9, bytes_accessed=10**7, transcendentals=0),
-    )(got.reshape(devices, 4 * LANES), first_weight)
+    )(got, first_weight)
     returned = lax.all_to_all(terms, AXES, split_axis=0, concat_axis=0, tiled=True)
     returned = returned.reshape(2 * devices, parts, LANES)
 
-    correlated = jnp.einsum(
-        "nj,vjk->nvk",
-        noise_draw,
-        panels[:, :, LANES : LANES + factor_rows],
-        preferred_element_type=jnp.float32,
-    ).reshape(docs_here, topics)
-    extra = correlated + head_bias
     scale = (128.0 * slot_count / doc_len.astype(jnp.float32))[:, None]
+    hidden = pl.pallas_call(
+        hidden_kernel,
+        out_shape=jax.ShapeDtypeStruct((docs_here, hidden_width), jnp.bfloat16),
+        in_specs=[SMEM, VMEM, VMEM, VMEM],
+        out_specs=VMEM,
+        scratch_shapes=[pltpu.VMEM((docs_here * parts, LANES), jnp.float32)],
+        compiler_params=PARAMS,
+        cost_estimate=pl.CostEstimate(flops=10**7, bytes_accessed=10**7, transcendentals=10**6),
+    )(place, returned, scale, first_bias.reshape(1, hidden_width))
     return pl.pallas_call(
-        finish_kernel,
+        output_kernel,
         out_shape=jax.ShapeDtypeStruct((docs_here, topics), jnp.bfloat16),
-        in_specs=[SMEM, VMEM, VMEM, VMEM, pl.BlockSpec(memory_space=pl.ANY), VMEM],
+        in_specs=[SMEM, VMEM, VMEM, pl.BlockSpec(memory_space=pl.ANY), VMEM],
         out_specs=VMEM,
         scratch_shapes=[
-            pltpu.VMEM((docs_here * parts, LANES), jnp.float32),
             pltpu.VMEM((vocab_devices, topics, LANES), jnp.bfloat16),
-            pltpu.SemaphoreType.DMA,
+            pltpu.VMEM((vocab_devices, topics, LANES), jnp.bfloat16),
+            pltpu.SemaphoreType.DMA((docs_devices,)),
+            pltpu.SemaphoreType.DMA((docs_devices,)),
         ],
         compiler_params=PARAMS,
-        cost_estimate=pl.CostEstimate(flops=10**9, bytes_accessed=10**7, transcendentals=10**6),
-    )(place, returned, scale, first_bias.reshape(1, hidden_width), panels, extra)
+        cost_estimate=pl.CostEstimate(flops=10**9, bytes_accessed=10**7, transcendentals=0),
+    )(shift, hidden, noise_draw, panels, head_bias.reshape(1, topics))
 
 
 def solution(mesh):
+    sizes = (8, 2, 4, 8)
+    fine = jax.sharding.Mesh(mesh.devices.reshape(sizes), AXES)
+    rows, vocab, docs = P(AXES), ("y", "core"), ("x", "z")
     return jax.shard_map(
         local,
-        mesh=mesh,
-        in_specs=(
-            P(("vocab", "docs"), None, None),
-            P(("vocab", "docs"), None),
-            P(("vocab", "docs"), None),
-            P(("vocab", "docs")),
-            P(("vocab", "docs"), None),
-            P(),
-            P("vocab", "docs"),
-            P(),
-            P("vocab", "docs"),
-            P(("vocab", "docs"), None),
-        ),
-        out_specs=P(("vocab", "docs"), None),
+        mesh=fine,
+        in_specs=(rows, rows, rows, rows, rows, P(), P(vocab, docs), P(), P(vocab, docs), rows),
+        out_specs=rows,
         check_vma=False,
     )

time: 246 us -> 230 us (0.935)
  waiting for transfers between devices: 143 us -> 117 us
  starting transfers between devices: 12.9 us -> 21.8 us
  Pallas kernels: 20.7 us -> 26.1 us
  matrix products: 4.6 us -> 0 us
    all_gather x1, waiting for transfers between devices: 143 us -> 0.72 us  [local(): lax.all_gather(jnp.concatenate(line, axis=0), ('y', 'core', 'z'), axis=0,...]
    all_to_all x1, waiting for transfers between devices: 0.01 us -> 116 us  [local(): lax.all_to_all(terms, AXES, split_axis=0, concat_axis=0, tiled=True)]
    ppermute x0 -> x3, starting transfers between devices: none -> 10.1 us  [local(): lax.ppermute(panel, 'x', [((i + k) % x_devices, i) for i in range(x_devic...]
    pallas_call x1 -> x2, Pallas kernels: 8.22 us -> 13.5 us  [the longest x1 8.65 us: local(): pl.pallas_call(output_kernel, out_shape=jax.ShapeDtypeStruct((docs_here,...]
    dot_general x1 -> x0, matrix products: 4.6 us -> none  [local(): jnp.einsum('nj,vjk->nvk', noise_draw, panels[:, :, LANES:LANES + factor_r...]
  transfers between devices with their start and end apart: 2 -> 5, of which waited for: 1 -> 2; matrix products, arithmetic and copies ran while one was open for 4% -> 2% of each run, Pallas kernels for 5% -> 8%
where the time goes in v2:
time: 230 us
  waiting for transfers between devices  117 us (51%)
  blocking collectives  45.2 us (20%)
  Pallas kernels  26.1 us (11%)
  starting transfers between devices  21.8 us (9%)
  between operations  13.5 us (6%)
  local copies, waits for them, and re-layouts  4.98 us (2%)
    all_to_all x1, waiting for transfers between devices, local(): lax.all_to_all(terms, AXES, split_axis=0, concat_axis=0, tiled=True)  116 us
    all_to_all x1, blocking collectives, local(): lax.all_to_all(send.reshape(devices, 4, LANES), AXES, split_axis=0, conca...  45.2 us
    all_to_all x1, starting transfers between devices, local(): lax.all_to_all(terms, AXES, split_axis=0, concat_axis=0, tiled=True)  11.7 us
    ppermute x3, starting transfers between devices, local(): lax.ppermute(panel, 'x', [((i + k) % x_devices, i) for i in range(x_devic...  10.1 us
    pallas_call x1, Pallas kernels, local(): pl.pallas_call(owner_kernel, out_shape=jax.ShapeDtypeStruct((devices, 2 *...  9.75 us
    pallas_call x1, Pallas kernels, local(): pl.pallas_call(output_kernel, out_shape=jax.ShapeDtypeStruct((docs_here,...  8.65 us
    pallas_call x1, Pallas kernels, local(): pl.pallas_call(hidden_kernel, out_shape=jax.ShapeDtypeStruct((docs_here,...  4.88 us
  transfers between devices with their start and end apart: 5, of which 2 were waited for; matrix products, arithmetic and copies ran while one was open for 2% of the time, Pallas kernels for 8%

profile of v2, /device:TPU:1, one launch (start us, length us, event | category | flops | bytes accessed | tf_op | source)
XLA Modules:
  0.0 230.0 jit_solution(4901663061957296913)
XLA Ops:
  6.5 0.0 all-gather.2.cloned.1.call-start
  6.5 0.7 fusion.1
  7.3 5.2 %collective-permute-start = (bf16[48,256]{1,0:T(8,128)(2,1)S(1)}, bf16[48,256]{1,0:T(8,128)(2,1)S(1)}, u32[]{:S(2)}, u32[]{:S(2)}) collective-permute-start(bf16[48,256]{1,0:T(8,128)(2,1)S(1)} %fusion.1), channel_id=1, source_target_pairs={{8,0},{16,8},{24,16},{0,24},{9,1},{17,9},{25,17},{1,25},{10,2},{18... | collective-permute-start | bytes 73736 | tf_op jit(solution)/shard_map/ppermute | solution.py:166
  12.5 2.4 %collective-permute-start.1 = (bf16[48,256]{1,0:T(8,128)(2,1)S(1)}, bf16[48,256]{1,0:T(8,128)(2,1)S(1)}, u32[]{:S(2)}, u32[]{:S(2)}) collective-permute-start(bf16[48,256]{1,0:T(8,128)(2,1)S(1)} %fusion.1), channel_id=1, source_target_pairs={{16,0},{24,8},{0,16},{8,24},{17,1},{25,9},{1,17},{9,25},{18,2},{26... | collective-permute-start | bytes 73736 | tf_op jit(solution)/shard_map/ppermute | solution.py:166
  14.9 2.5 %collective-permute-start.2 = (bf16[48,256]{1,0:T(8,128)(2,1)S(1)}, bf16[48,256]{1,0:T(8,128)(2,1)S(1)}, u32[]{:S(2)}, u32[]{:S(2)}) collective-permute-start(bf16[48,256]{1,0:T(8,128)(2,1)S(1)} %fusion.1), channel_id=1, source_target_pairs={{24,0},{0,8},{8,16},{16,24},{25,1},{1,9},{9,17},{17,25},{26,2},{2,... | collective-permute-start | bytes 73736 | tf_op jit(solution)/shard_map/ppermute | solution.py:166
  17.4 1.6 copy.11
  19.0 2.8 %shard_map.100 = (bf16[512,512]{1,0:T(8,128)(2,1)}, s32[1,512]{1,0:T(1,128)}) custom-call(s32[1,512]{1,0:T(1,128)} %bitcast.28, s32[1,512]{1,0:T(1,128)} %bitcast.29, bf16[512,128]{1,0:T(8,128)(2,1)} %bitcast.24), custom_call_target="tpu_custom_call" | custom-call | flops 1000000000 | bytes 1000000 | tf_op jit(solution)/shard_map/pallas_call | solution.py:170
  21.8 0.0 collective-permute-done
  21.8 0.0 collective-permute-done.1
  21.8 0.0 collective-permute-done.2
  21.8 0.6 pad_maximum_fusion
  22.5 0.0 all-gather.2.cloned.1.call-update
  22.5 1.2 reshape.34
  23.7 45.2 %all_to_all.10 = bf16[512,4,128]{2,1,0:T(4,128)(2,1)S(1)} all-to-all(bf16[512,4,128]{2,1,0:T(4,128)(2,1)S(1)} %reshape.34), channel_id=1, replica_groups=mesh['y'=8,'core'=2,'x'=4,'z'=8] {'y','core','x','z'}, dimensions={0} | all-to-all | bytes 1048576 | tf_op jit(solution)/shard_map/all_to_all | solution.py:186
  68.9 0.9 copy.15
  69.8 9.7 %shard_map.101 = bf16[512,32,128]{2,1,0:T(8,128)(2,1)} custom-call(bf16[512,512]{1,0:T(8,128)(2,1)} %bitcast.22, bf16[1024,2048]{1,0:T(8,128)(2,1)} %weight_ref.1), custom_call_target="tpu_custom_call" | custom-call | flops 5000000000 | bytes 10000000 | tf_op jit(solution)/shard_map/pallas_call | solution.py:190
  79.5 0.0 copy-start.1
  79.5 0.0 copy-start
  79.5 11.7 %all-to-all-start.1 = ((bf16[512,32,128]{2,1,0:T(8,128)(2,1)}), bf16[512,32,128]{2,1,0:T(8,128)(2,1)}, u32[]{:S(2)}, u32[]{:S(2)}) async-start(bf16[512,32,128]{2,1,0:T(8,128)(2,1)} %shard_map.101), calls=%async_computation.1 | async-start | bytes 8388608 | tf_op jit(solution)/shard_map/all_to_all | solution.py:202
  91.2 0.0 copy-done.1
  91.2 0.7 copy.12.scale_ref
  91.9 0.0 copy-done
  91.9 0.6 reshape.39.bias_ref
  92.6 116.3 %all-to-all-done.1 = bf16[512,32,128]{2,1,0:T(8,128)(2,1)} async-done(((bf16[512,32,128]{2,1,0:T(8,128)(2,1)}), bf16[512,32,128]{2,1,0:T(8,128)(2,1)}, u32[]{:S(2)}, u32[]{:S(2)}) %all-to-all-start.1) | async-done | bytes 4194336 | tf_op jit(solution)/shard_map/all_to_all | solution.py:202
  208.9 4.9 %shard_map.102.hidden_ref = bf16[128,2048]{1,0:T(8,128)(2,1)} custom-call(s32[1,512]{1,0:T(1,128)} %get-tuple-element.12.place_ref, bf16[1024,16,128]{2,1,0:T(8,128)(2,1)} %bitcast.9.got_ref, f32[128,1]{1,0:T(8,128)} %copy.12.scale_ref, f32[1,2048]{1,0:T(1,128)} %bitcast.27), custom_call_target="tpu_custom_call" | custom-call | flops 10000000 | bytes 10000000 | tf_op jit(solution)/shard_map/pallas_call | solution.py:206
  213.8 0.7 all-gather.2.cloned.1.call-done
  214.5 8.7 %shard_map.103 = bf16[128,1536]{1,0:T(8,128)(2,1)} custom-call(s32[1]{0:T(128)} %bitcast.shift_ref, bf16[128,2048]{1,0:T(8,128)(2,1)} %shard_map.102.hidden_ref, bf16[128,1536]{1,0:T(8,128)(2,1)} %noise_ref.1, bf16[16,8,4,48,256]{4,3,2,1,0:T(8,128)(2,1)} %bitcast.20, f32[1,1536]{1,0:T(1,128)} %reshape.39.bias_ref), custom_call_target="tpu_custom_call" | custom-call | flops 1000000000 | bytes 10000000 | tf_op jit(solution)/shard_map/pallas_call | solution.py:215
  (1 shorter events, 0.0 us)
Async XLA Ops:
  6.5 208.0 %all-gather.2.cloned.1.call-start = ((), (), s32[]{:S(2)}) async-start(), calls=%async_computation.2 | async-start | bytes 12681216 | tf_op jit(solution)/shard_map/all_gather | solution.py:182
  7.3 14.6 %collective-permute-start = (bf16[48,256]{1,0:T(8,128)(2,1)S(1)}, bf16[48,256]{1,0:T(8,128)(2,1)S(1)}, u32[]{:S(2)}, u32[]{:S(2)}) collective-permute-start(bf16[48,256]{1,0:T(8,128)(2,1)S(1)} %fusion.1), channel_id=1, source_target_pairs={{8,0},{16,8},{24,16},{0,24},{9,1},{17,9},{25,17},{1,25},{10,2},{18... | collective-permute-start | bytes 73736 | tf_op jit(solution)/shard_map/ppermute | solution.py:166
  12.5 9.3 %collective-permute-start.1 = (bf16[48,256]{1,0:T(8,128)(2,1)S(1)}, bf16[48,256]{1,0:T(8,128)(2,1)S(1)}, u32[]{:S(2)}, u32[]{:S(2)}) collective-permute-start(bf16[48,256]{1,0:T(8,128)(2,1)S(1)} %fusion.1), channel_id=1, source_target_pairs={{16,0},{24,8},{0,16},{8,24},{17,1},{25,9},{1,17},{9,25},{18,2},{26... | collective-permute-start | bytes 73736 | tf_op jit(solution)/shard_map/ppermute | solution.py:166
  14.9 6.9 %collective-permute-start.2 = (bf16[48,256]{1,0:T(8,128)(2,1)S(1)}, bf16[48,256]{1,0:T(8,128)(2,1)S(1)}, u32[]{:S(2)}, u32[]{:S(2)}) collective-permute-start(bf16[48,256]{1,0:T(8,128)(2,1)S(1)} %fusion.1), channel_id=1, source_target_pairs={{24,0},{0,8},{8,16},{16,24},{25,1},{1,9},{9,17},{17,25},{26,2},{2,... | collective-permute-start | bytes 73736 | tf_op jit(solution)/shard_map/ppermute | solution.py:166
  79.5 11.7 %copy-start.1 = (s32[128]{0:T(128)S(1)}, s32[128]{0:T(128)}, u32[]{:S(2)}) copy-start(s32[128]{0:T(128)} %param.13) | copy-start | bytes 1540
  79.5 12.4 %copy-start = (f32[1536]{0:T(1024)S(1)}, f32[1536]{0:T(1024)}, u32[]{:S(2)}) copy-start(f32[1536]{0:T(1024)} %param.17) | copy-start | bytes 18436
  79.5 129.4 %all-to-all-start.1 = ((bf16[512,32,128]{2,1,0:T(8,128)(2,1)}), bf16[512,32,128]{2,1,0:T(8,128)(2,1)}, u32[]{:S(2)}, u32[]{:S(2)}) async-start(bf16[512,32,128]{2,1,0:T(8,128)(2,1)} %shard_map.101), calls=%async_computation.1 | async-start | bytes 8388608 | tf_op jit(solution)/shard_map/all_to_all | solution.py:202
Sparse Core Ops, SparseCore 0:
  22.6 191.8 all-gather.1

commit v3 on v2

--- a/solution.py
+++ b/solution.py
@@ -13,9 +13,9 @@
 NT = (((1,), (1,)), ((), ()))
 
 
-def route_kernel(owner_ref, sub_ref, rows_ref, send_ref, place_ref):
+def route_kernel(owner_ref, sub_ref, rows_ref, send_ref, place_ref, stage):
     slots = owner_ref.shape[1]
-    devices = send_ref.shape[0]
+    devices = send_ref.shape[0] // 4
     owner = owner_ref[...]
     named = owner == lax.broadcasted_iota(jnp.int32, (devices, slots), 0)
     named_b = jnp.where(named, 1.0, 0.0).astype(jnp.bfloat16)
@@ -34,29 +34,42 @@
     sub = jnp.broadcast_to(sub_ref[...].astype(jnp.float32), (LANES, slots)).astype(jnp.bfloat16)
     picks = (jnp.where(named & (before < 0.5), 1.0, 0.0).astype(jnp.bfloat16), second.astype(jnp.bfloat16))
     for p, pick in enumerate(picks):
-        send_ref[:, p * LANES : (p + 1) * LANES] = jnp.dot(
+        stage[pl.ds(p, devices, stride=4), :] = jnp.dot(
             pick, rows, preferred_element_type=jnp.float32
-        ).astype(jnp.bfloat16)
-        send_ref[:, (2 + p) * LANES : (3 + p) * LANES] = lax.dot_general(
+        )
+        stage[pl.ds(2 + p, devices, stride=4), :] = lax.dot_general(
             pick, sub, NT, preferred_element_type=jnp.float32
-        ).astype(jnp.bfloat16)
-
-
-def owner_kernel(got_ref, weight_ref, out_ref, spread, stage):
-    devices = got_ref.shape[0]
+        )
+    send_ref[...] = stage[...].astype(jnp.bfloat16)
+
+
+def owner_kernel(got_ref, weight_hbm, out_ref, spread, stage, rows_stage, weight_ref, sem):
+    width = 256
+    copies = [
+        pltpu.make_async_copy(
+            weight_hbm.at[:, pl.ds(k * width, width)],
+            weight_ref.at[:, pl.ds(k * width, width)],
+            sem.at[k],
+        )
+        for k in range(weight_ref.shape[1] // width)
+    ]
+    for copy in copies:
+        copy.start()
+    devices = got_ref.shape[0] // 4
     blocks = weight_ref.shape[0] // LANES
+    rows_stage[...] = got_ref[...].astype(jnp.float32)
     parts = weight_ref.shape[1] // LANES
     for p in range(2):
-        rows = got_ref[:, p * LANES : (p + 1) * LANES]
-        sub = got_ref[:, (2 + p) * LANES : (3 + p) * LANES].astype(jnp.float32)
+        rows = rows_stage[pl.ds(p, devices, stride=4), :]
+        sub = rows_stage[pl.ds(2 + p, devices, stride=4), :]
         for b in range(blocks):
             spread[p * devices : (p + 1) * devices, b * LANES : (b + 1) * LANES] = jnp.where(
-                sub == float(b), rows.astype(jnp.float32), 0.0
+                sub == float(b), rows, 0.0
             ).astype(jnp.bfloat16)
-    width = 256
     for g in range(parts // 8):
         for cc in range(8 * LANES // width):
             column = g * 8 * LANES + cc * width
+            copies[column // width].wait()
             terms = jnp.dot(
                 spread[...], weight_ref[:, column : column + width], preferred_element_type=jnp.float32
             )
@@ -170,11 +183,12 @@
     send, place = pl.pallas_call(
         route_kernel,
         out_shape=(
-            jax.ShapeDtypeStruct((devices, 4 * LANES), jnp.bfloat16),
+            jax.ShapeDtypeStruct((devices * 4, LANES), jnp.bfloat16),
             jax.ShapeDtypeStruct((1, slots), jnp.int32),
         ),
         in_specs=[VMEM] * 3,
         out_specs=(VMEM, VMEM),
+        scratch_shapes=[pltpu.VMEM((devices * 4, LANES), jnp.float32)],
         compiler_params=PARAMS,
         cost_estimate=pl.CostEstimate(flops=10**9, bytes_accessed=10**6, transcendentals=0),
     )(owner_flat, sub_flat, rows)
@@ -186,15 +200,18 @@
     got = lax.all_to_all(
         send.reshape(devices, 4, LANES), AXES, split_axis=0, concat_axis=0, tiled=True
     )
-    got = got.reshape(devices, 4 * LANES)
+    got = got.reshape(devices * 4, LANES)
     terms = pl.pallas_call(
         owner_kernel,
         out_shape=jax.ShapeDtypeStruct((devices, 2 * parts, LANES), jnp.bfloat16),
-        in_specs=[VMEM] * 2,
+        in_specs=[VMEM, pl.BlockSpec(memory_space=pl.ANY)],
         out_specs=VMEM,
         scratch_shapes=[
             pltpu.VMEM((2 * devices, first_weight.shape[0]), jnp.bfloat16),
             pltpu.VMEM((2, devices * 8, LANES), jnp.float32),
+            pltpu.VMEM((devices * 4, LANES), jnp.float32),
+            pltpu.VMEM(first_weight.shape, jnp.bfloat16),
+            pltpu.SemaphoreType.DMA((hidden_width // 256,)),
         ],
         compiler_params=PARAMS,
         cost_estimate=pl.CostEstimate(flops=5 * 10**9, bytes_accessed=10**7, transcendentals=0),

time: 230 us -> 232 us (level)
  Pallas kernels: 26.1 us -> 31.1 us
    pallas_call x1, Pallas kernels: 9.75 us -> 14.8 us  [local(): pl.pallas_call(owner_kernel, out_shape=jax.ShapeDtypeStruct((devices, 2 *...]
  transfers between devices with their start and end apart: 5 -> 5, of which waited for: 2 -> 1; matrix products, arithmetic and copies ran while one was open for 2% -> 1% of each run, Pallas kernels for 8% -> 10%
where the time goes in v3:
time: 232 us
  waiting for transfers between devices  116 us (50%)
  blocking collectives  44 us (19%)
  Pallas kernels  31.1 us (13%)
  starting transfers between devices  23.3 us (10%)
  between operations  13.5 us (6%)
  local copies, waits for them, and re-layouts  2.93 us (1%)
    all_to_all x1, waiting for transfers between devices, local(): lax.all_to_all(terms, AXES, split_axis=0, concat_axis=0, tiled=True)  116 us
    all_to_all x1, blocking collectives, local(): lax.all_to_all(send.reshape(devices, 4, LANES), AXES, split_axis=0, conca...  44 us
    pallas_call x1, Pallas kernels, local(): pl.pallas_call(owner_kernel, out_shape=jax.ShapeDtypeStruct((devices, 2 *...  14.8 us
    all_to_all x1, starting transfers between devices, local(): lax.all_to_all(terms, AXES, split_axis=0, concat_axis=0, tiled=True)  13.2 us
    ppermute x3, starting transfers between devices, local(): lax.ppermute(panel, 'x', [((i + k) % x_devices, i) for i in range(x_devic...  10.1 us
    pallas_call x1, Pallas kernels, local(): pl.pallas_call(output_kernel, out_shape=jax.ShapeDtypeStruct((docs_here,...  8.66 us
    pallas_call x1, Pallas kernels, local(): pl.pallas_call(hidden_kernel, out_shape=jax.ShapeDtypeStruct((docs_here,...  4.81 us
  transfers between devices with their start and end apart: 5, of which 1 were waited for; matrix products, arithmetic and copies ran while one was open for 1% of the time, Pallas kernels for 10%

profile of v3, /device:TPU:1, one launch (start us, length us, event | category | flops | bytes accessed | tf_op | source)
XLA Modules:
  0.0 232.0 jit_solution(1727308701310584070)
XLA Ops:
  6.5 0.0 all-gather.2.cloned.1.call-start
  6.5 0.7 fusion.1
  7.3 5.2 %collective-permute-start = (bf16[48,256]{1,0:T(8,128)(2,1)S(1)}, bf16[48,256]{1,0:T(8,128)(2,1)S(1)}, u32[]{:S(2)}, u32[]{:S(2)}) collective-permute-start(bf16[48,256]{1,0:T(8,128)(2,1)S(1)} %fusion.1), channel_id=1, source_target_pairs={{8,0},{16,8},{24,16},{0,24},{9,1},{17,9},{25,17},{1,25},{10,2},{18... | collective-permute-start | bytes 73736 | tf_op jit(solution)/shard_map/ppermute | solution.py:179
  12.5 2.4 %collective-permute-start.1 = (bf16[48,256]{1,0:T(8,128)(2,1)S(1)}, bf16[48,256]{1,0:T(8,128)(2,1)S(1)}, u32[]{:S(2)}, u32[]{:S(2)}) collective-permute-start(bf16[48,256]{1,0:T(8,128)(2,1)S(1)} %fusion.1), channel_id=1, source_target_pairs={{16,0},{24,8},{0,16},{8,24},{17,1},{25,9},{1,17},{9,25},{18,2},{26... | collective-permute-start | bytes 73736 | tf_op jit(solution)/shard_map/ppermute | solution.py:179
  14.9 2.5 %collective-permute-start.2 = (bf16[48,256]{1,0:T(8,128)(2,1)S(1)}, bf16[48,256]{1,0:T(8,128)(2,1)S(1)}, u32[]{:S(2)}, u32[]{:S(2)}) collective-permute-start(bf16[48,256]{1,0:T(8,128)(2,1)S(1)} %fusion.1), channel_id=1, source_target_pairs={{24,0},{0,8},{8,16},{16,24},{25,1},{1,9},{9,17},{17,25},{26,2},{2,... | collective-permute-start | bytes 73736 | tf_op jit(solution)/shard_map/ppermute | solution.py:179
  17.4 1.6 copy.11
  19.0 2.9 %shard_map.100 = (bf16[2048,128]{1,0:T(8,128)(2,1)}, s32[1,512]{1,0:T(1,128)}) custom-call(s32[1,512]{1,0:T(1,128)} %bitcast.26, s32[1,512]{1,0:T(1,128)} %bitcast.27, bf16[512,128]{1,0:T(8,128)(2,1)} %bitcast.22), custom_call_target="tpu_custom_call" | custom-call | flops 1000000000 | bytes 1000000 | tf_op jit(solution)/shard_map/pallas_call | solution.py:183
  21.9 0.0 collective-permute-done
  21.9 0.0 collective-permute-done.1
  21.9 0.0 collective-permute-done.2
  21.9 0.6 pad_maximum_fusion
  22.5 0.0 all-gather.2.cloned.1.call-update
  22.6 44.0 %all_to_all.10 = bf16[512,4,128]{2,1,0:T(4,128)(2,1)} all-to-all(bf16[512,4,128]{2,1,0:T(4,128)(2,1)} %bitcast.19), channel_id=1, replica_groups=mesh['y'=8,'core'=2,'x'=4,'z'=8] {'y','core','x','z'}, dimensions={0} | all-to-all | bytes 1048576 | tf_op jit(solution)/shard_map/all_to_all | solution.py:200
  66.6 14.8 %shard_map.101 = bf16[512,32,128]{2,1,0:T(8,128)(2,1)} custom-call(bf16[2048,128]{1,0:T(8,128)(2,1)} %bitcast.20, bf16[1024,2048]{1,0:T(8,128)(2,1)} %weight_hbm.1), custom_call_target="tpu_custom_call" | custom-call | flops 5000000000 | bytes 10000000 | tf_op jit(solution)/shard_map/pallas_call | solution.py:204
  81.4 0.0 copy-start.1
  81.4 0.0 copy-start
  81.4 13.2 %all-to-all-start.1 = ((bf16[512,32,128]{2,1,0:T(8,128)(2,1)}), bf16[512,32,128]{2,1,0:T(8,128)(2,1)}, u32[]{:S(2)}, u32[]{:S(2)}) async-start(bf16[512,32,128]{2,1,0:T(8,128)(2,1)} %shard_map.101), calls=%async_computation.1 | async-start | bytes 8388608 | tf_op jit(solution)/shard_map/all_to_all | solution.py:219
  94.6 0.0 copy-done.1
  94.6 0.7 copy.12.scale_ref
  95.4 0.0 copy-done
  95.4 0.6 reshape.39.bias_ref
  96.0 115.7 %all-to-all-done.1 = bf16[512,32,128]{2,1,0:T(8,128)(2,1)} async-done(((bf16[512,32,128]{2,1,0:T(8,128)(2,1)}), bf16[512,32,128]{2,1,0:T(8,128)(2,1)}, u32[]{:S(2)}, u32[]{:S(2)}) %all-to-all-start.1) | async-done | bytes 4194336 | tf_op jit(solution)/shard_map/all_to_all | solution.py:219
  211.6 4.8 %shard_map.102.hidden_ref = bf16[128,2048]{1,0:T(8,128)(2,1)} custom-call(s32[1,512]{1,0:T(1,128)} %get-tuple-element.12.place_ref, bf16[1024,16,128]{2,1,0:T(8,128)(2,1)} %bitcast.11.got_ref, f32[128,1]{1,0:T(8,128)} %copy.12.scale_ref, f32[1,2048]{1,0:T(1,128)} %bitcast.25), custom_call_target="tpu_custom_call" | custom-call | flops 10000000 | bytes 10000000 | tf_op jit(solution)/shard_map/pallas_call | solution.py:223
  216.5 0.0 all-gather.2.cloned.1.call-done
  216.5 8.7 %shard_map.103 = bf16[128,1536]{1,0:T(8,128)(2,1)} custom-call(s32[1]{0:T(128)} %bitcast.shift_ref, bf16[128,2048]{1,0:T(8,128)(2,1)} %shard_map.102.hidden_ref, bf16[128,1536]{1,0:T(8,128)(2,1)} %noise_ref.1, bf16[16,8,4,48,256]{4,3,2,1,0:T(8,128)(2,1)} %bitcast.18, f32[1,1536]{1,0:T(1,128)} %reshape.39.bias_ref), custom_call_target="tpu_custom_call" | custom-call | flops 1000000000 | bytes 10000000 | tf_op jit(solution)/shard_map/pallas_call | solution.py:232
  (1 shorter events, 0.0 us)
Async XLA Ops:
  6.5 209.9 %all-gather.2.cloned.1.call-start = ((), (), s32[]{:S(2)}) async-start(), calls=%async_computation.2 | async-start | bytes 12681216 | tf_op jit(solution)/shard_map/all_gather | solution.py:196
  7.3 14.6 %collective-permute-start = (bf16[48,256]{1,0:T(8,128)(2,1)S(1)}, bf16[48,256]{1,0:T(8,128)(2,1)S(1)}, u32[]{:S(2)}, u32[]{:S(2)}) collective-permute-start(bf16[48,256]{1,0:T(8,128)(2,1)S(1)} %fusion.1), channel_id=1, source_target_pairs={{8,0},{16,8},{24,16},{0,24},{9,1},{17,9},{25,17},{1,25},{10,2},{18... | collective-permute-start | bytes 73736 | tf_op jit(solution)/shard_map/ppermute | solution.py:179
  12.5 9.4 %collective-permute-start.1 = (bf16[48,256]{1,0:T(8,128)(2,1)S(1)}, bf16[48,256]{1,0:T(8,128)(2,1)S(1)}, u32[]{:S(2)}, u32[]{:S(2)}) collective-permute-start(bf16[48,256]{1,0:T(8,128)(2,1)S(1)} %fusion.1), channel_id=1, source_target_pairs={{16,0},{24,8},{0,16},{8,24},{17,1},{25,9},{1,17},{9,25},{18,2},{26... | collective-permute-start | bytes 73736 | tf_op jit(solution)/shard_map/ppermute | solution.py:179
  14.9 7.0 %collective-permute-start.2 = (bf16[48,256]{1,0:T(8,128)(2,1)S(1)}, bf16[48,256]{1,0:T(8,128)(2,1)S(1)}, u32[]{:S(2)}, u32[]{:S(2)}) collective-permute-start(bf16[48,256]{1,0:T(8,128)(2,1)S(1)} %fusion.1), channel_id=1, source_target_pairs={{24,0},{0,8},{8,16},{16,24},{25,1},{1,9},{9,17},{17,25},{26,2},{2,... | collective-permute-start | bytes 73736 | tf_op jit(solution)/shard_map/ppermute | solution.py:179
  81.4 13.2 %copy-start.1 = (s32[128]{0:T(128)S(1)}, s32[128]{0:T(128)}, u32[]{:S(2)}) copy-start(s32[128]{0:T(128)} %param.13) | copy-start | bytes 1540
  81.4 13.9 %copy-start = (f32[1536]{0:T(1024)S(1)}, f32[1536]{0:T(1024)}, u32[]{:S(2)}) copy-start(f32[1536]{0:T(1024)} %param.17) | copy-start | bytes 18436
  81.4 130.2 %all-to-all-start.1 = ((bf16[512,32,128]{2,1,0:T(8,128)(2,1)}), bf16[512,32,128]{2,1,0:T(8,128)(2,1)}, u32[]{:S(2)}, u32[]{:S(2)}) async-start(bf16[512,32,128]{2,1,0:T(8,128)(2,1)} %shard_map.101), calls=%async_computation.1 | async-start | bytes 8388608 | tf_op jit(solution)/shard_map/all_to_all | solution.py:219
Sparse Core Ops, SparseCore 0:
  22.7 190.3 all-gather.1
